TPU v7x, 32 devices: a whole 2x2x4 slice. The times are simulated.
32 devices in a mesh: groups: 2 (over x), row: 16 (over z, y, core).
Axes of the slice: x: 2, y: 2, z: 4, core: 2. Of those that a mesh axis runs over, the one named last changes fastest.
Arguments:
- basis: float32 [8192, 128], P(('groups', 'row')), parts along dimension 0, may hold values from -6 to 6
- springs: float32 [8192], P(('groups', 'row')), parts along dimension 0, may hold values from 0.25 to 8
- tangent_blocks: float32 [4096, 4096], P(('groups', 'row')), parts along dimension 0, may hold values from -0.375 to 0.375
- tile_rows: int32 [4096], P(('groups', 'row')), parts along dimension 0, may hold values from 0 to 3
- tile_owner: int32 [4096, 1], P(('groups', 'row')), parts along dimension 0, may hold values from 0 to 15, as said below
- tile_offset: int32 [4096], P(('groups', 'row')), parts along dimension 0, may hold values from 0 to 3
- tile_count: int32 [32], P(('groups', 'row')), parts along dimension 0, may hold values from 32 to 128, as said below
Outputs:
- stiff_image: float32 [8192, 128], P(('groups', 'row')), parts along dimension 0
- reduced: float32 [256, 128], P('groups'), parts along dimension 0
There are 2 independent parts, one for each index of `groups`. A program takes and returns all parts, laid end to end along the dimension named above; each array names one. Nothing has to cross between parts.
Inputs may be any that keep to these rules, and one draw needn't show every extreme that they name: The first tile_count[d] slots of device d are live; some device has exactly 128. `tile_owner`: the slab is closed into a shell: every slot of device d names owner (d + o) mod 16 with o one of 0, 1, -1, 4, -4, 5, -5, 8. Among the slots of one device no owner appears more than 32 times, and owner d itself appears exactly 32 times in every device.
All inputs are finite; a program needn't handle non-finite values.
Results may differ from a plain program's by a relative error of at most 0.0003.
Values sent between devices are 32-bit elements; how exact they have to be, the bound alone decides.
No kernel may reach another device: no remote copies, remote signals or barrier semaphores. Data moves between devices by JAX's collectives and lax.ppermute only.
A program may use at most 128 MiB of HBM per device.

v0:
```python
import functools

import jax
import jax.numpy as jnp
from jax import lax
from jax.experimental import pallas as pl
from jax.experimental.pallas import tpu as pltpu
from jax.sharding import PartitionSpec as P

B = 64
MODES = 128
BR_DEV = 4
CAP = 128
LINKS = 8
LATE = 3
HALF = B // 2
ROWS = BR_DEV * B


def split(x):
    high = x.astype(jnp.bfloat16)
    return high, (x - high.astype(jnp.float32)).astype(jnp.bfloat16)


def dot3(a_high, a_low, b_high, b_low):
    dot = functools.partial(jnp.dot, preferred_element_type=jnp.float32)
    return dot(a_high, b_high) + (dot(a_low, b_high) + dot(a_high, b_low))


def halves():
    for r in range(BR_DEV):
        for h in range(2):
            yield pl.ds(r * B + h, HALF, stride=2), slice(r * B + h * HALF, r * B + (h + 1) * HALF)


def assemble(place_ref, count_ref, blocks_ref, basis_ref, high_ref, low_ref, turned_high_ref, turned_low_ref, weight_high_ref, weight_low_ref, slots, dense, sorted_basis):
    dense[...] = jnp.zeros_like(dense)
    for rows, target in halves():
        sorted_basis[target, :] = basis_ref[rows, :]
    turned_high, turned_low = split(sorted_basis[...].T)
    turned_high_ref[...] = turned_high
    turned_low_ref[...] = turned_low

    @pl.loop(0, CAP // 8)
    def _(group):
        eight = blocks_ref[pl.ds(pl.multiple_of(group * 8, 8), 8), :]
        for t in range(HALF):
            slots[pl.ds(group * (8 * HALF) + t, 8, stride=HALF), :] = eight[:, t * 128:(t + 1) * 128]

    @pl.loop(0, count_ref[0])
    def _(s):
        target = pl.ds(pl.multiple_of(place_ref[s] * HALF, HALF), HALF)
        dense[target, :] += slots[pl.ds(pl.multiple_of(s * HALF, HALF), HALF), :]

    left = lax.broadcasted_iota(jnp.int32, (HALF, 128), 1) < B

    @pl.loop(0, LINKS)
    def _(link):
        for r in range(BR_DEV):
            for pair in range(BR_DEV // 2):
                start = ((link * BR_DEV + r) * BR_DEV + 2 * pair) * HALF
                first = dense[pl.ds(pl.multiple_of(start, HALF), HALF), :]
                second = dense[pl.ds(pl.multiple_of(start + HALF, HALF), HALF), :]
                even = jnp.where(left, first, pltpu.roll(second, B, 1))
                odd = jnp.where(left, pltpu.roll(first, B, 1), second)
                for h, part in enumerate((even, odd)):
                    high, low = split(part)
                    rows = slice(r * B + h * HALF, r * B + (h + 1) * HALF)
                    high_ref[link, rows, pair * 128:(pair + 1) * 128] = high
                    low_ref[link, rows, pair * 128:(pair + 1) * 128] = low

    for k in range(LATE):
        link = LINKS - LATE + k
        high, low = split(dot3(turned_high, turned_low, high_ref[link], low_ref[link]))
        weight_high_ref[k] = high
        weight_low_ref[k] = low


def project_early(high_ref, low_ref, turned_high_ref, turned_low_ref, springs_ref, own_ref, *refs):
    basis_refs, (total_ref, partial_ref) = refs[:-2], refs[-2:]
    total = jnp.zeros((ROWS, MODES), jnp.float32)
    for link, ref in enumerate((own_ref,) + basis_refs):
        b_high, b_low = split(ref[...])
        total += dot3(high_ref[link], low_ref[link], b_high, b_low)
    for part in range(ROWS // MODES):
        rows = slice(part * MODES, (part + 1) * MODES)
        column = jnp.broadcast_to(springs_ref[:, rows], (MODES, MODES)).T
        total_ref[rows, :] = column * own_ref[rows, :]
    for rows, target in halves():
        total_ref[rows, :] += total[target, :]
    sorted_total = jnp.concatenate([total_ref[rows, :] for rows, _ in halves()], axis=0)
    partial_ref[...] = dot3(turned_high_ref[...], turned_low_ref[...], *split(sorted_total))


def reduce_late(scale, weight_high_ref, weight_low_ref, early_ref, *refs):
    basis_refs, partial_ref = refs[:LATE], refs[LATE]
    total = early_ref[...]
    for k, ref in enumerate(basis_refs):
        total += dot3(weight_high_ref[k], weight_low_ref[k], *split(ref[...]))
    partial_ref[...] = total * scale


def add_after(first_ref, second_ref, done_ref, sum_ref):
    sum_ref[...] = first_ref[...] + second_ref[...]


def choose(core_ref, odd_ref, even_ref, whole_ref):
    @pl.when(core_ref[0] == 1)
    def _():
        whole_ref[...] = odd_ref[...]

    @pl.when(core_ref[0] == 0)
    def _():
        whole_ref[...] = even_ref[...]


def project_late(high_ref, low_ref, total_ref, *refs):
    basis_refs, (stiff_ref, done_ref) = refs[:LATE], refs[LATE:]
    total = jnp.zeros((ROWS, MODES), jnp.float32)
    for k, ref in enumerate(basis_refs):
        b_high, b_low = split(ref[...])
        total += dot3(high_ref[LINKS - LATE + k], low_ref[LINKS - LATE + k], b_high, b_low)
    for rows, target in halves():
        stiff_ref[rows, :] = total_ref[rows, :] + total[target, :]
    done_ref[...] = jnp.zeros_like(done_ref)


def shards(basis, springs, tangent_blocks, tile_rows, tile_owner, tile_offset, tile_count):
    n = lax.axis_size("row")
    me = lax.axis_index("row")
    steps = (0, 1, n - 1, 4, n - 4, n // 2, 5, n - 5)

    def fetch(block, step):
        return lax.ppermute(block, "row", [((d + step) % n, d) for d in range(n)])

    above, below = fetch(basis, 4), fetch(basis, n - 4)
    across = fetch(basis, n // 2)
    after, before = fetch(basis, 1), fetch(basis, n - 1)
    far_above, far_below = fetch(above, 1), fetch(below, n - 1)

    away = (tile_owner[:, 0] - me + n) % n
    link = jnp.zeros_like(away)
    for k, step in enumerate(steps):
        link = jnp.where(away == step, k, link)
    place = (link * BR_DEV + tile_rows) * BR_DEV + tile_offset

    smem = pl.BlockSpec(memory_space=pltpu.SMEM)
    vmem = pl.BlockSpec(memory_space=pltpu.VMEM)
    half, full = jnp.bfloat16, jnp.float32
    params = pltpu.CompilerParams(vmem_limit_bytes=32 * 2**20)

    high, low, turned_high, turned_low, weight_high, weight_low = pl.pallas_call(
        assemble,
        out_shape=(
            jax.ShapeDtypeStruct((LINKS, ROWS, ROWS), half),
            jax.ShapeDtypeStruct((LINKS, ROWS, ROWS), half),
            jax.ShapeDtypeStruct((MODES, ROWS), half),
            jax.ShapeDtypeStruct((MODES, ROWS), half),
            jax.ShapeDtypeStruct((LATE, MODES, ROWS), half),
            jax.ShapeDtypeStruct((LATE, MODES, ROWS), half),
        ),
        in_specs=[smem, smem, vmem, vmem],
        out_specs=(vmem,) * 6,
        scratch_shapes=[
            pltpu.VMEM((CAP * HALF, 128), full),
            pltpu.VMEM((CAP * HALF, 128), full),
            pltpu.VMEM((ROWS, MODES), full),
        ],
        compiler_params=params,
        cost_estimate=pl.CostEstimate(flops=10_000_000, bytes_accessed=12_000_000, transcendentals=0),
        name="assemble",
    )(place, tile_count, tangent_blocks, basis)

    total, early = pl.pallas_call(
        project_early,
        out_shape=(jax.ShapeDtypeStruct((ROWS, MODES), full), jax.ShapeDtypeStruct((MODES, MODES), full)),
        in_specs=[vmem] * (5 + LINKS - LATE),
        out_specs=(vmem,) * 2,
        compiler_params=params,
        cost_estimate=pl.CostEstimate(flops=300_000_000, bytes_accessed=2_500_000, transcendentals=0),
        name="project_early",
    )(high, low, turned_high, turned_low, springs.reshape(1, ROWS), basis, after, before, above, below)

    square = jax.ShapeDtypeStruct((MODES, MODES), full)
    partial = pl.pallas_call(
        functools.partial(reduce_late, 1.0 / (basis.shape[0] * n)),
        out_shape=square,
        in_specs=[vmem] * (3 + LATE),
        out_specs=vmem,
        compiler_params=params,
        cost_estimate=pl.CostEstimate(flops=80_000_000, bytes_accessed=700_000, transcendentals=0),
        name="reduce_late",
    )(weight_high, weight_low, early, across, far_above, far_below)

    stiff_image, done = pl.pallas_call(
        project_late,
        out_shape=(jax.ShapeDtypeStruct((ROWS, MODES), full), jax.ShapeDtypeStruct((8, 128), full)),
        in_specs=[vmem] * (3 + LATE),
        out_specs=(vmem,) * 2,
        compiler_params=params,
        cost_estimate=pl.CostEstimate(flops=160_000_000, bytes_accessed=1_500_000, transcendentals=0),
        name="project_late",
    )(high, low, total, across, far_above, far_below)

    def swap(block, apart):
        return lax.ppermute(block, "row", [(d, d ^ apart) for d in range(1, n, 2)])

    mine = partial + lax.ppermute(partial, "row", [(d, d + 1) for d in range(0, n, 2)])
    apart = 2
    if n.bit_length() % 2:
        mine = pl.pallas_call(
            add_after,
            out_shape=square,
            in_specs=[vmem] * 3,
            out_specs=vmem,
            compiler_params=params,
            name="add_after",
        )(mine, swap(mine, apart), done)
        apart *= 2
    while apart < n:
        pair = mine + swap(mine, apart)
        mine = pair + (swap(mine, 2 * apart) + swap(mine, 3 * apart))
        apart *= 4
    back = lax.ppermute(mine, "row", [(d, d - 1) for d in range(1, n, 2)])
    reduced = pl.pallas_call(
        choose,
        out_shape=square,
        in_specs=[smem, vmem, vmem],
        out_specs=vmem,
        compiler_params=params,
        cost_estimate=pl.CostEstimate(flops=0, bytes_accessed=130_000, transcendentals=0),
        name="choose",
    )((me % 2).reshape(1), mine, back)
    return (stiff_image, reduced)


def solution(mesh):
    in_specs = (
        P(("groups", "row"), None),
        P(("groups", "row")),
        P(("groups", "row"), None),
        P(("groups", "row")),
        P(("groups", "row"), None),
        P(("groups", "row")),
        P(("groups", "row")),
    )
    out_specs = (P(("groups", "row"), None), P("groups", None))
    return jax.shard_map(shards, mesh=mesh, in_specs=in_specs, out_specs=out_specs, check_vma=False)
```

profile of v0, /device:TPU:0, one launch (start us, length us, event | category | flops | bytes accessed | tf_op | source)
XLA Modules:
  0.0 47.1 jit_solution(13165561293130144555)
XLA Ops:
  0.6 5.1 %collective-permute-start.2 = (f32[256,128]{1,0:T(8,128)}, f32[256,128]{1,0:T(8,128)S(1)}, u32[]{:S(2)}, u32[]{:S(2)}) collective-permute-start(f32[256,128]{1,0:T(8,128)} %own_ref.1), channel_id=1, source_target_pairs={{4,0},{5,1},{6,2},{7,3},{8,4},{9,5},{10,6},{11,7},{12,8},{13,9},{1... | collective-permute-start | bytes 393224 | tf_op jit(solution)/shard_map/ppermute | solution.py:134
  5.7 0.0 collective-permute-start.3
  5.7 3.7 %collective-permute-start = (f32[256,128]{1,0:T(8,128)}, f32[256,128]{1,0:T(8,128)S(1)}, u32[]{:S(2)}, u32[]{:S(2)}) collective-permute-start(f32[256,128]{1,0:T(8,128)} %own_ref.1), channel_id=1, source_target_pairs={{1,0},{2,1},{3,2},{4,3},{5,4},{6,5},{7,6},{8,7},{9,8},{10,9},{11,1... | collective-permute-start | bytes 393224 | tf_op jit(solution)/shard_map/ppermute | solution.py:134
  9.4 0.0 collective-permute-start.1
  9.4 0.0 collective-permute-start.4
  9.4 0.6 %collective-permute-done.2.refs_2_ = f32[256,128]{1,0:T(8,128)S(1)} collective-permute-done((f32[256,128]{1,0:T(8,128)}, f32[256,128]{1,0:T(8,128)S(1)}, u32[]{:S(2)}, u32[]{:S(2)}) %collective-permute-start.2) | collective-permute-done | bytes 131104 | tf_op jit(solution)/shard_map/ppermute | solution.py:134
  10.0 3.9 %collective-permute-start.5 = (f32[256,128]{1,0:T(8,128)S(1)}, f32[256,128]{1,0:T(8,128)S(1)}, u32[]{:S(2)}, u32[]{:S(2)}) collective-permute-start(f32[256,128]{1,0:T(8,128)S(1)} %collective-permute-done.2.refs_2_), channel_id=1, source_target_pairs={{1,0},{2,1},{3,2},{4,3},{5,4},{6,5},{7,6},{8,7},{9,8},{10,9},{11,1... | collective-permute-start | bytes 393224 | tf_op jit(solution)/shard_map/ppermute | solution.py:134
  13.9 0.0 collective-permute-done.3.refs_3_
  13.9 0.0 collective-permute-start.6
  13.9 0.7 %multiply_add_fusion.place_ref = s32[128]{0:T(128)S(1)} fusion(s32[128]{0:T(128)} %param.12, s32[128]{0:T(128)} %param.10, s32[128,1]{0,1:T(1,128)} %param.11, s32[]{:T(128)S(6)} %axis_index.12), kind=kLoop, calls=%fused_computation.14 | loop fusion | flops 3968 | bytes 2052 | tf_op jit(solution)/shard_map/add | solution.py:145
  15.2 0.0 copy-start
  15.2 1.6 %copy-done = f32[128,4096]{1,0:T(8,128)S(1)} copy-done((f32[128,4096]{1,0:T(8,128)S(1)}, f32[128,4096]{1,0:T(8,128)}, u32[]{:S(2)}) %copy-start) | copy-done | bytes 2097176
  16.8 0.9 %copy-done.1 = f32[256,128]{1,0:T(8,128)S(1)} copy-done((f32[256,128]{1,0:T(8,128)S(1)}, f32[256,128]{1,0:T(8,128)}, u32[]{:S(2)}) %copy-start.1) | copy-done | bytes 131096
  17.7 4.1 %assemble.1 = (bf16[8,256,256]{2,1,0:T(8,128)(2,1)S(1)}, bf16[8,256,256]{2,1,0:T(8,128)(2,1)S(1)}, bf16[128,256]{1,0:T(8,128)(2,1)S(1)}, bf16[128,256]{1,0:T(8,1...) custom-call(s32[128]{0:T(128)S(1)} %multiply_add_fusion.place_ref, s32[1]{0:T(128)S(6)} %copy.9.count_ref, ...), custom_call_target="tpu_custom_call" | custom-call | flops 10000000 | bytes 12000000 | tf_op jit(solution)/shard_map/assemble/pallas_call | solution.py:152
  21.8 0.0 collective-permute-done.refs_0_
  21.8 0.0 collective-permute-done.1.refs_1_
  21.9 0.9 %project_early.1 = (f32[256,128]{1,0:T(8,128)S(1)}, f32[128,128]{1,0:T(8,128)S(1)}) custom-call(bf16[8,256,256]{2,1,0:T(8,128)(2,1)S(1)} %get-tuple-element.12.high_ref, bf16[8,256,256]{2,1,0:T(8,128)(2,1)S(1)} %get-tuple-element.13.low_ref, bf16[128,256]{1,0:T(8,128)(2,1)S(1)} %get-tuple-element.14.turned_high_ref, ...), custom_call_target="tpu_custom_call" | custom-call | flops 300000000 | bytes 2500000 | tf_op jit(solution)/shard_map/project_early/pallas_call | solution.py:174
  22.8 0.0 collective-permute-done.6.refs_2_
  22.8 0.3 reduce_late.1
  23.1 2.4 %collective-permute-start.7 = (f32[128,128]{1,0:T(8,128)S(1)}, f32[128,128]{1,0:T(8,128)S(1)}, u32[]{:S(2)}, u32[]{:S(2)}) collective-permute-start(f32[128,128]{1,0:T(8,128)S(1)} %reduce_late.1), channel_id=1, source_target_pairs={{0,1},{2,3},{4,5},{6,7},{8,9},{10,11},{12,13},{14,15},{16,17},{18,... | collective-permute-start | bytes 196616 | tf_op jit(solution)/shard_map/ppermute | solution.py:208
  25.6 0.9 %collective-permute-done.7 = f32[128,128]{1,0:T(8,128)S(1)} collective-permute-done((f32[128,128]{1,0:T(8,128)S(1)}, f32[128,128]{1,0:T(8,128)S(1)}, u32[]{:S(2)}, u32[]{:S(2)}) %collective-permute-start.7) | collective-permute-done | bytes 65568 | tf_op jit(solution)/shard_map/ppermute | solution.py:208
  26.4 0.7 %collective-permute-start.8 = (f32[128,128]{1,0:T(8,128)S(1)}, f32[128,128]{1,0:T(8,128)S(1)}, u32[]{:S(2)}, u32[]{:S(2)}) collective-permute-start(f32[128,128]{1,0:T(8,128)S(1)} %add.47.first_ref), channel_id=1, source_target_pairs={{1,3},{3,1},{5,7},{7,5},{9,11},{11,9},{13,15},{15,13},{17,19},{19,... | collective-permute-start | bytes 196616 | tf_op jit(solution)/shard_map/ppermute | solution.py:206
  27.1 1.1 %project_late.1 = (f32[256,128]{1,0:T(8,128)}, f32[8,128]{1,0:T(8,128)S(1)}) custom-call(bf16[8,256,256]{2,1,0:T(8,128)(2,1)S(1)} %get-tuple-element.12.high_ref, bf16[8,256,256]{2,1,0:T(8,128)(2,1)S(1)} %get-tuple-element.13.low_ref, f32[256,128]{1,0:T(8,128)S(1)} %get-tuple-element.16.total_ref, f32[256,128]{1,0:T(8,128)S(1)} %collective-permute-done.4.refs_0_, ...), custom_call_target="tpu_custom_call" | custom-call | flops 160000000 | bytes 1500000 | tf_op jit(solution)/shard_map/project_late/pallas_call | solution.py:195
  28.2 0.0 collective-permute-done.8.second_ref
  28.3 0.7 %collective-permute-start.10 = (f32[128,128]{1,0:T(8,128)S(1)}, f32[128,128]{1,0:T(8,128)S(1)}, u32[]{:S(2)}, u32[]{:S(2)}) collective-permute-start(f32[128,128]{1,0:T(8,128)S(1)} %add_after.1), channel_id=1, source_target_pairs={{1,9},{3,11},{5,13},{7,15},{9,1},{11,3},{13,5},{15,7},{17,25},{19,... | collective-permute-start | bytes 196616 | tf_op jit(solution)/shard_map/ppermute | solution.py:206
  28.9 0.7 %collective-permute-start.11 = (f32[128,128]{1,0:T(8,128)S(1)}, f32[128,128]{1,0:T(8,128)S(1)}, u32[]{:S(2)}, u32[]{:S(2)}) collective-permute-start(f32[128,128]{1,0:T(8,128)S(1)} %add_after.1), channel_id=1, source_target_pairs={{1,13},{3,15},{5,9},{7,11},{9,5},{11,7},{13,1},{15,3},{17,29},{19,... | collective-permute-start | bytes 196616 | tf_op jit(solution)/shard_map/ppermute | solution.py:206
  29.6 0.7 %collective-permute-start.9 = (f32[128,128]{1,0:T(8,128)S(1)}, f32[128,128]{1,0:T(8,128)S(1)}, u32[]{:S(2)}, u32[]{:S(2)}) collective-permute-start(f32[128,128]{1,0:T(8,128)S(1)} %add_after.1), channel_id=1, source_target_pairs={{1,5},{3,7},{5,1},{7,3},{9,13},{11,15},{13,9},{15,11},{17,21},{19,... | collective-permute-start | bytes 196616 | tf_op jit(solution)/shard_map/ppermute | solution.py:206
  30.3 0.0 collective-permute-done.11
  30.3 0.0 collective-permute-done.9
  30.3 1.3 %collective-permute-start.12 = (f32[128,128]{1,0:T(8,128)S(1)}, f32[128,128]{1,0:T(8,128)S(1)}, u32[]{:S(2)}, u32[]{:S(2)}) collective-permute-start(f32[128,128]{1,0:T(8,128)S(1)} %add_add_fusion.odd_ref), channel_id=1, source_target_pairs={{1,0},{3,2},{5,4},{7,6},{9,8},{11,10},{13,12},{15,14},{17,16},{19,... | collective-permute-start | bytes 196616 | tf_op jit(solution)/shard_map/ppermute | solution.py:224
  31.7 14.8 %collective-permute-done.12.even_ref = f32[128,128]{1,0:T(8,128)S(1)} collective-permute-done((f32[128,128]{1,0:T(8,128)S(1)}, f32[128,128]{1,0:T(8,128)S(1)}, u32[]{:S(2)}, u32[]{:S(2)}) %collective-permute-start.12) | collective-permute-done | bytes 65568 | tf_op jit(solution)/shard_map/ppermute | solution.py:224
  46.5 0.6 %choose.1 = f32[128,128]{1,0:T(8,128)} custom-call(s32[1]{0:T(128)} %bitcast.2.core_ref, f32[128,128]{1,0:T(8,128)S(1)} %add_add_fusion.odd_ref, f32[128,128]{1,0:T(8,128)S(1)} %collective-permute-done.12.even_ref), custom_call_target="tpu_custom_call" | custom-call | bytes 130000 | tf_op jit(solution)/shard_map/choose/pallas_call | solution.py:225
  (11 shorter events, 0.1 us)
Async XLA Ops:
  0.6 21.2 %copy-start.3 = (f32[256]{0:T(256)S(1)}, f32[256]{0:T(256)}, u32[]{:S(2)}) copy-start(f32[256]{0:T(256)} %param.8) | copy-start | bytes 3076
  0.6 9.3 %collective-permute-start.2 = (f32[256,128]{1,0:T(8,128)}, f32[256,128]{1,0:T(8,128)S(1)}, u32[]{:S(2)}, u32[]{:S(2)}) collective-permute-start(f32[256,128]{1,0:T(8,128)} %own_ref.1), channel_id=1, source_target_pairs={{4,0},{5,1},{6,2},{7,3},{8,4},{9,5},{10,6},{11,7},{12,8},{13,9},{1... | collective-permute-start | bytes 393224 | tf_op jit(solution)/shard_map/ppermute | solution.py:134
  5.7 8.1 %collective-permute-start.3 = (f32[256,128]{1,0:T(8,128)}, f32[256,128]{1,0:T(8,128)S(1)}, u32[]{:S(2)}, u32[]{:S(2)}) collective-permute-start(f32[256,128]{1,0:T(8,128)} %own_ref.1), channel_id=1, source_target_pairs={{12,0},{13,1},{14,2},{15,3},{0,4},{1,5},{2,6},{3,7},{4,8},{5,9},{6... | collective-permute-start | bytes 393224 | tf_op jit(solution)/shard_map/ppermute | solution.py:134
  5.7 16.1 %collective-permute-start = (f32[256,128]{1,0:T(8,128)}, f32[256,128]{1,0:T(8,128)S(1)}, u32[]{:S(2)}, u32[]{:S(2)}) collective-permute-start(f32[256,128]{1,0:T(8,128)} %own_ref.1), channel_id=1, source_target_pairs={{1,0},{2,1},{3,2},{4,3},{5,4},{6,5},{7,6},{8,7},{9,8},{10,9},{11,1... | collective-permute-start | bytes 393224 | tf_op jit(solution)/shard_map/ppermute | solution.py:134
  9.4 12.4 %collective-permute-start.1 = (f32[256,128]{1,0:T(8,128)}, f32[256,128]{1,0:T(8,128)S(1)}, u32[]{:S(2)}, u32[]{:S(2)}) collective-permute-start(f32[256,128]{1,0:T(8,128)} %own_ref.1), channel_id=1, source_target_pairs={{15,0},{0,1},{1,2},{2,3},{3,4},{4,5},{5,6},{6,7},{7,8},{8,9},{9,10... | collective-permute-start | bytes 393224 | tf_op jit(solution)/shard_map/ppermute | solution.py:134
  9.4 13.4 %collective-permute-start.4 = (f32[256,128]{1,0:T(8,128)}, f32[256,128]{1,0:T(8,128)S(1)}, u32[]{:S(2)}, u32[]{:S(2)}) collective-permute-start(f32[256,128]{1,0:T(8,128)} %own_ref.1), channel_id=1, source_target_pairs={{8,0},{9,1},{10,2},{11,3},{12,4},{13,5},{14,6},{15,7},{0,8},{1,9},... | collective-permute-start | bytes 393224 | tf_op jit(solution)/shard_map/ppermute | solution.py:134
  10.0 12.8 %collective-permute-start.5 = (f32[256,128]{1,0:T(8,128)S(1)}, f32[256,128]{1,0:T(8,128)S(1)}, u32[]{:S(2)}, u32[]{:S(2)}) collective-permute-start(f32[256,128]{1,0:T(8,128)S(1)} %collective-permute-done.2.refs_2_), channel_id=1, source_target_pairs={{1,0},{2,1},{3,2},{4,3},{5,4},{6,5},{7,6},{8,7},{9,8},{10,9},{11,1... | collective-permute-start | bytes 393224 | tf_op jit(solution)/shard_map/ppermute | solution.py:134
  13.9 8.9 %collective-permute-start.6 = (f32[256,128]{1,0:T(8,128)S(1)}, f32[256,128]{1,0:T(8,128)S(1)}, u32[]{:S(2)}, u32[]{:S(2)}) collective-permute-start(f32[256,128]{1,0:T(8,128)S(1)} %collective-permute-done.3.refs_3_), channel_id=1, source_target_pairs={{15,0},{0,1},{1,2},{2,3},{3,4},{4,5},{5,6},{6,7},{7,8},{8,9},{9,10... | collective-permute-start | bytes 393224 | tf_op jit(solution)/shard_map/ppermute | solution.py:134
  15.2 1.6 %copy-start = (f32[128,4096]{1,0:T(8,128)S(1)}, f32[128,4096]{1,0:T(8,128)}, u32[]{:S(2)}) copy-start(f32[128,4096]{1,0:T(8,128)} %blocks_ref.1) | copy-start | bytes 6291460
  16.8 0.9 %copy-start.1 = (f32[256,128]{1,0:T(8,128)S(1)}, f32[256,128]{1,0:T(8,128)}, u32[]{:S(2)}) copy-start(f32[256,128]{1,0:T(8,128)} %own_ref.1) | copy-start | bytes 393220
  17.7 4.1 %copy-start.2 = (f32[256,128]{1,0:T(8,128)S(1)}, f32[256,128]{1,0:T(8,128)}, u32[]{:S(2)}) copy-start(f32[256,128]{1,0:T(8,128)} %own_ref.1) | copy-start | bytes 393220
  23.1 3.3 %collective-permute-start.7 = (f32[128,128]{1,0:T(8,128)S(1)}, f32[128,128]{1,0:T(8,128)S(1)}, u32[]{:S(2)}, u32[]{:S(2)}) collective-permute-start(f32[128,128]{1,0:T(8,128)S(1)} %reduce_late.1), channel_id=1, source_target_pairs={{0,1},{2,3},{4,5},{6,7},{8,9},{10,11},{12,13},{14,15},{16,17},{18,... | collective-permute-start | bytes 196616 | tf_op jit(solution)/shard_map/ppermute | solution.py:208
  26.4 1.8 %collective-permute-start.8 = (f32[128,128]{1,0:T(8,128)S(1)}, f32[128,128]{1,0:T(8,128)S(1)}, u32[]{:S(2)}, u32[]{:S(2)}) collective-permute-start(f32[128,128]{1,0:T(8,128)S(1)} %add.47.first_ref), channel_id=1, source_target_pairs={{1,3},{3,1},{5,7},{7,5},{9,11},{11,9},{13,15},{15,13},{17,19},{19,... | collective-permute-start | bytes 196616 | tf_op jit(solution)/shard_map/ppermute | solution.py:206
  28.3 2.0 %collective-permute-start.10 = (f32[128,128]{1,0:T(8,128)S(1)}, f32[128,128]{1,0:T(8,128)S(1)}, u32[]{:S(2)}, u32[]{:S(2)}) collective-permute-start(f32[128,128]{1,0:T(8,128)S(1)} %add_after.1), channel_id=1, source_target_pairs={{1,9},{3,11},{5,13},{7,15},{9,1},{11,3},{13,5},{15,7},{17,25},{19,... | collective-permute-start | bytes 196616 | tf_op jit(solution)/shard_map/ppermute | solution.py:206
  28.9 1.4 %collective-permute-start.11 = (f32[128,128]{1,0:T(8,128)S(1)}, f32[128,128]{1,0:T(8,128)S(1)}, u32[]{:S(2)}, u32[]{:S(2)}) collective-permute-start(f32[128,128]{1,0:T(8,128)S(1)} %add_after.1), channel_id=1, source_target_pairs={{1,13},{3,15},{5,9},{7,11},{9,5},{11,7},{13,1},{15,3},{17,29},{19,... | collective-permute-start | bytes 196616 | tf_op jit(solution)/shard_map/ppermute | solution.py:206
  29.6 0.7 %collective-permute-start.9 = (f32[128,128]{1,0:T(8,128)S(1)}, f32[128,128]{1,0:T(8,128)S(1)}, u32[]{:S(2)}, u32[]{:S(2)}) collective-permute-start(f32[128,128]{1,0:T(8,128)S(1)} %add_after.1), channel_id=1, source_target_pairs={{1,5},{3,7},{5,1},{7,3},{9,13},{11,15},{13,9},{15,11},{17,21},{19,... | collective-permute-start | bytes 196616 | tf_op jit(solution)/shard_map/ppermute | solution.py:206
  30.3 16.1 %collective-permute-start.12 = (f32[128,128]{1,0:T(8,128)S(1)}, f32[128,128]{1,0:T(8,128)S(1)}, u32[]{:S(2)}, u32[]{:S(2)}) collective-permute-start(f32[128,128]{1,0:T(8,128)S(1)} %add_add_fusion.odd_ref), channel_id=1, source_target_pairs={{1,0},{3,2},{5,4},{7,6},{9,8},{11,10},{13,12},{15,14},{17,16},{19,... | collective-permute-start | bytes 196616 | tf_op jit(solution)/shard_map/ppermute | solution.py:224
where the time goes:
time: 47.5 us; the launch traced here: 47.1 us
  starting transfers between devices  19 us (40%)
  waiting for transfers between devices  16.3 us (34%)
  Pallas kernels  7.09 us (15%)
  local copies, waits for them, and re-layouts  2.5 us (5%)
  between operations  1.48 us (3%)
  other arithmetic  0.74 us (2%)
    ppermute x1, waiting for transfers between devices, shards(): back = lax.ppermute(mine, 'row', [(d, d - 1) for d in range(1, n, 2)])  14.8 us
    ppermute x7, starting transfers between devices, fetch(): return lax.ppermute(block, 'row', [((d + step) % n, d) for d in range(n)])  12.7 us
    pallas_call x1, Pallas kernels, shards(): pl.pallas_call(assemble, out_shape=(jax.ShapeDtypeStruct((LINKS, ROWS, RO...  4.09 us
    ppermute x4, starting transfers between devices, swap(): return lax.ppermute(block, 'row', [(d, d ^ apart) for d in range(1, n, 2)])  2.66 us
    unnamed x8, local copies, waits for them, and re-layouts  2.5 us
    ppermute x1, starting transfers between devices, shards(): lax.ppermute(partial, 'row', [(d, d + 1) for d in range(0, n, 2)])  2.42 us
    ppermute x1, starting transfers between devices, shards(): back = lax.ppermute(mine, 'row', [(d, d - 1) for d in range(1, n, 2)])  1.29 us
    pallas_call x1, Pallas kernels, shards(): pl.pallas_call(project_late, out_shape=(jax.ShapeDtypeStruct((ROWS, MODES...  1.13 us
  transfers between devices with their start and end apart: 13, of which 3 were waited for; matrix products, arithmetic and copies ran while one was open for 2% of the time, Pallas kernels for 13%

commit v1 on v0

--- a/solution.py
+++ b/solution.py
@@ -203,25 +203,22 @@
     )(high, low, total, across, far_above, far_below)
 
     def swap(block, apart):
-        return lax.ppermute(block, "row", [(d, d ^ apart) for d in range(1, n, 2)])
-
-    mine = partial + lax.ppermute(partial, "row", [(d, d + 1) for d in range(0, n, 2)])
-    apart = 2
-    if n.bit_length() % 2:
-        mine = pl.pallas_call(
-            add_after,
-            out_shape=square,
-            in_specs=[vmem] * 3,
-            out_specs=vmem,
-            compiler_params=params,
-            name="add_after",
-        )(mine, swap(mine, apart), done)
+        return lax.ppermute(block, "row", [(d, d ^ apart if apart == 1 or d % 2 else d) for d in range(n)])
+
+    mine = partial + swap(partial, 1)
+    mine = pl.pallas_call(
+        add_after,
+        out_shape=square,
+        in_specs=[vmem] * 3,
+        out_specs=vmem,
+        compiler_params=params,
+        name="add_after",
+    )(mine, swap(mine, 2), done)
+    apart = 4
+    while apart < n:
+        mine += swap(mine, apart)
         apart *= 2
-    while apart < n:
-        pair = mine + swap(mine, apart)
-        mine = pair + (swap(mine, 2 * apart) + swap(mine, 3 * apart))
-        apart *= 4
-    back = lax.ppermute(mine, "row", [(d, d - 1) for d in range(1, n, 2)])
+    back = swap(mine, 1)
     reduced = pl.pallas_call(
         choose,
         out_shape=square,

time: 47.5 us -> 43.5 us (0.916)
  waiting for transfers between devices: 16.3 us -> 2.38 us
  starting transfers between devices: 19 us -> 29.3 us
    ppermute x6 -> x5, waiting for transfers between devices: 15.7 us -> 1.81 us  [swap(): lax.ppermute(block, 'row', [(d, d ^ apart if apart == 1 or d % 2 else d)...]
    ppermute x6 -> x5, starting transfers between devices: 6.37 us -> 16.7 us  [swap(): lax.ppermute(block, 'row', [(d, d ^ apart if apart == 1 or d % 2 else d)...]
  transfers between devices with their start and end apart: 13 -> 12, of which waited for: 3 -> 3; matrix products, arithmetic and copies ran while one was open for 2% -> 2% of each run, Pallas kernels for 13% -> 14%
where the time goes in v1:
time: 43.5 us; the launch traced here: 43.3 us
  starting transfers between devices  29.3 us (67%)
  Pallas kernels  6.91 us (16%)
  local copies, waits for them, and re-layouts  2.5 us (6%)
  waiting for transfers between devices  2.38 us (5%)
  between operations  1.45 us (3%)
  other arithmetic  0.74 us (2%)
    ppermute x5, starting transfers between devices, swap(): lax.ppermute(block, 'row', [(d, d ^ apart if apart == 1 or d % 2 else d)...  16.7 us
    ppermute x7, starting transfers between devices, fetch(): return lax.ppermute(block, 'row', [((d + step) % n, d) for d in range(n)])  12.7 us
    pallas_call x1, Pallas kernels, shards(): pl.pallas_call(assemble, out_shape=(jax.ShapeDtypeStruct((LINKS, ROWS, RO...  3.91 us
    unnamed x8, local copies, waits for them, and re-layouts  2.5 us
    ppermute x5, waiting for transfers between devices, swap(): lax.ppermute(block, 'row', [(d, d ^ apart if apart == 1 or d % 2 else d)...  1.81 us
    pallas_call x1, Pallas kernels, shards(): pl.pallas_call(project_late, out_shape=(jax.ShapeDtypeStruct((ROWS, MODES...  1.13 us
    pallas_call x1, Pallas kernels, shards(): pl.pallas_call(project_early, out_shape=(jax.ShapeDtypeStruct((ROWS, MODE...  0.91 us
  transfers between devices with their start and end apart: 12, of which 3 were waited for; matrix products, arithmetic and copies ran while one was open for 2% of the time, Pallas kernels for 14%

profile of v1, /device:TPU:0, one launch (start us, length us, event | category | flops | bytes accessed | tf_op | source)
XLA Modules:
  0.0 43.3 jit_solution(1428094869903173227)
XLA Ops:
  0.6 5.1 %collective-permute-start.2 = (f32[256,128]{1,0:T(8,128)}, f32[256,128]{1,0:T(8,128)S(1)}, u32[]{:S(2)}, u32[]{:S(2)}) collective-permute-start(f32[256,128]{1,0:T(8,128)} %own_ref.1), channel_id=1, source_target_pairs={{4,0},{5,1},{6,2},{7,3},{8,4},{9,5},{10,6},{11,7},{12,8},{13,9},{1... | collective-permute-start | bytes 393224 | tf_op jit(solution)/shard_map/ppermute | solution.py:134
  5.7 0.0 collective-permute-start.3
  5.7 3.7 %collective-permute-start = (f32[256,128]{1,0:T(8,128)}, f32[256,128]{1,0:T(8,128)S(1)}, u32[]{:S(2)}, u32[]{:S(2)}) collective-permute-start(f32[256,128]{1,0:T(8,128)} %own_ref.1), channel_id=1, source_target_pairs={{1,0},{2,1},{3,2},{4,3},{5,4},{6,5},{7,6},{8,7},{9,8},{10,9},{11,1... | collective-permute-start | bytes 393224 | tf_op jit(solution)/shard_map/ppermute | solution.py:134
  9.4 0.0 collective-permute-start.1
  9.4 0.0 collective-permute-start.4
  9.4 0.6 %collective-permute-done.2.refs_2_ = f32[256,128]{1,0:T(8,128)S(1)} collective-permute-done((f32[256,128]{1,0:T(8,128)}, f32[256,128]{1,0:T(8,128)S(1)}, u32[]{:S(2)}, u32[]{:S(2)}) %collective-permute-start.2) | collective-permute-done | bytes 131104 | tf_op jit(solution)/shard_map/ppermute | solution.py:134
  10.0 3.9 %collective-permute-start.5 = (f32[256,128]{1,0:T(8,128)S(1)}, f32[256,128]{1,0:T(8,128)S(1)}, u32[]{:S(2)}, u32[]{:S(2)}) collective-permute-start(f32[256,128]{1,0:T(8,128)S(1)} %collective-permute-done.2.refs_2_), channel_id=1, source_target_pairs={{1,0},{2,1},{3,2},{4,3},{5,4},{6,5},{7,6},{8,7},{9,8},{10,9},{11,1... | collective-permute-start | bytes 393224 | tf_op jit(solution)/shard_map/ppermute | solution.py:134
  13.9 0.0 collective-permute-done.3.refs_3_
  13.9 0.0 collective-permute-start.6
  13.9 0.7 %multiply_add_fusion.place_ref = s32[128]{0:T(128)S(1)} fusion(s32[128]{0:T(128)} %param.12, s32[128]{0:T(128)} %param.10, s32[128,1]{0,1:T(1,128)} %param.11, s32[]{:T(128)S(6)} %axis_index.12), kind=kLoop, calls=%fused_computation.13 | loop fusion | flops 3968 | bytes 2052 | tf_op jit(solution)/shard_map/add | solution.py:145
  15.2 0.0 copy-start
  15.2 1.6 %copy-done = f32[128,4096]{1,0:T(8,128)S(1)} copy-done((f32[128,4096]{1,0:T(8,128)S(1)}, f32[128,4096]{1,0:T(8,128)}, u32[]{:S(2)}) %copy-start) | copy-done | bytes 2097176
  16.8 0.9 %copy-done.1 = f32[256,128]{1,0:T(8,128)S(1)} copy-done((f32[256,128]{1,0:T(8,128)S(1)}, f32[256,128]{1,0:T(8,128)}, u32[]{:S(2)}) %copy-start.1) | copy-done | bytes 131096
  17.7 3.9 %assemble.1 = (bf16[8,256,256]{2,1,0:T(8,128)(2,1)S(1)}, bf16[8,256,256]{2,1,0:T(8,128)(2,1)S(1)}, bf16[128,256]{1,0:T(8,128)(2,1)S(1)}, bf16[128,256]{1,0:T(8,1...) custom-call(s32[128]{0:T(128)S(1)} %multiply_add_fusion.place_ref, s32[1]{0:T(128)S(6)} %copy.9.count_ref, ...), custom_call_target="tpu_custom_call" | custom-call | flops 10000000 | bytes 12000000 | tf_op jit(solution)/shard_map/assemble/pallas_call | solution.py:152
  21.6 0.0 collective-permute-done.refs_0_
  21.6 0.0 collective-permute-done.1.refs_1_
  21.7 0.9 %project_early.1 = (f32[256,128]{1,0:T(8,128)S(1)}, f32[128,128]{1,0:T(8,128)S(1)}) custom-call(bf16[8,256,256]{2,1,0:T(8,128)(2,1)S(1)} %get-tuple-element.12.high_ref, bf16[8,256,256]{2,1,0:T(8,128)(2,1)S(1)} %get-tuple-element.13.low_ref, bf16[128,256]{1,0:T(8,128)(2,1)S(1)} %get-tuple-element.14.turned_high_ref, ...), custom_call_target="tpu_custom_call" | custom-call | flops 300000000 | bytes 2500000 | tf_op jit(solution)/shard_map/project_early/pallas_call | solution.py:174
  22.6 0.0 collective-permute-done.4.refs_0_
  22.6 0.0 collective-permute-done.5.refs_1_
  22.6 0.0 collective-permute-done.6.refs_2_
  22.6 0.3 reduce_late.1
  23.0 0.7 %collective-permute-start.7 = (f32[128,128]{1,0:T(8,128)S(1)}, f32[128,128]{1,0:T(8,128)S(1)}, u32[]{:S(2)}, u32[]{:S(2)}) collective-permute-start(f32[128,128]{1,0:T(8,128)S(1)} %reduce_late.1), channel_id=1, source_target_pairs={{0,1},{1,0},{2,3},{3,2},{4,5},{5,4},{6,7},{7,6},{8,9},{9,8},{10,11... | collective-permute-start | bytes 196616 | tf_op jit(solution)/shard_map/ppermute | solution.py:206
  23.7 0.9 %collective-permute-done.7 = f32[128,128]{1,0:T(8,128)S(1)} collective-permute-done((f32[128,128]{1,0:T(8,128)S(1)}, f32[128,128]{1,0:T(8,128)S(1)}, u32[]{:S(2)}, u32[]{:S(2)}) %collective-permute-start.7) | collective-permute-done | bytes 65568 | tf_op jit(solution)/shard_map/ppermute | solution.py:206
  24.6 0.7 %collective-permute-start.8 = (f32[128,128]{1,0:T(8,128)S(1)}, f32[128,128]{1,0:T(8,128)S(1)}, u32[]{:S(2)}, u32[]{:S(2)}) collective-permute-start(f32[128,128]{1,0:T(8,128)S(1)} %add.44.first_ref), channel_id=1, source_target_pairs={{0,0},{1,3},{2,2},{3,1},{4,4},{5,7},{6,6},{7,5},{8,8},{9,11},{10,1... | collective-permute-start | bytes 196616 | tf_op jit(solution)/shard_map/ppermute | solution.py:206
  25.3 1.1 %project_late.1 = (f32[256,128]{1,0:T(8,128)}, f32[8,128]{1,0:T(8,128)S(1)}) custom-call(bf16[8,256,256]{2,1,0:T(8,128)(2,1)S(1)} %get-tuple-element.12.high_ref, bf16[8,256,256]{2,1,0:T(8,128)(2,1)S(1)} %get-tuple-element.13.low_ref, f32[256,128]{1,0:T(8,128)S(1)} %get-tuple-element.16.total_ref, f32[256,128]{1,0:T(8,128)S(1)} %collective-permute-done.4.refs_0_, ...), custom_call_target="tpu_custom_call" | custom-call | flops 160000000 | bytes 1500000 | tf_op jit(solution)/shard_map/project_late/pallas_call | solution.py:195
  26.4 0.0 collective-permute-done.8.second_ref
  26.4 0.7 %collective-permute-start.9 = (f32[128,128]{1,0:T(8,128)S(1)}, f32[128,128]{1,0:T(8,128)S(1)}, u32[]{:S(2)}, u32[]{:S(2)}) collective-permute-start(f32[128,128]{1,0:T(8,128)S(1)} %add_after.1), channel_id=1, source_target_pairs={{0,0},{1,5},{2,2},{3,7},{4,4},{5,1},{6,6},{7,3},{8,8},{9,13},{10,1... | collective-permute-start | bytes 196616 | tf_op jit(solution)/shard_map/ppermute | solution.py:206
  27.1 0.0 collective-permute-done.9
  27.1 0.7 %collective-permute-start.10 = (f32[128,128]{1,0:T(8,128)S(1)}, f32[128,128]{1,0:T(8,128)S(1)}, u32[]{:S(2)}, u32[]{:S(2)}) collective-permute-start(f32[128,128]{1,0:T(8,128)S(1)} %add.45), channel_id=1, source_target_pairs={{0,0},{1,9},{2,2},{3,11},{4,4},{5,13},{6,6},{7,15},{8,8},{9,1},{10... | collective-permute-start | bytes 196616 | tf_op jit(solution)/shard_map/ppermute | solution.py:206
  27.8 13.9 %collective-permute-start.11 = (f32[128,128]{1,0:T(8,128)S(1)}, f32[128,128]{1,0:T(8,128)S(1)}, u32[]{:S(2)}, u32[]{:S(2)}) collective-permute-start(f32[128,128]{1,0:T(8,128)S(1)} %add.46.odd_ref), channel_id=1, source_target_pairs={{0,1},{1,0},{2,3},{3,2},{4,5},{5,4},{6,7},{7,6},{8,9},{9,8},{10,11... | collective-permute-start | bytes 196616 | tf_op jit(solution)/shard_map/ppermute | solution.py:206
  41.8 0.9 %collective-permute-done.11.even_ref = f32[128,128]{1,0:T(8,128)S(1)} collective-permute-done((f32[128,128]{1,0:T(8,128)S(1)}, f32[128,128]{1,0:T(8,128)S(1)}, u32[]{:S(2)}, u32[]{:S(2)}) %collective-permute-start.11) | collective-permute-done | bytes 65568 | tf_op jit(solution)/shard_map/ppermute | solution.py:206
  42.7 0.6 %choose.1 = f32[128,128]{1,0:T(8,128)} custom-call(s32[1]{0:T(128)} %bitcast.2.core_ref, f32[128,128]{1,0:T(8,128)S(1)} %add.46.odd_ref, f32[128,128]{1,0:T(8,128)S(1)} %collective-permute-done.11.even_ref), custom_call_target="tpu_custom_call" | custom-call | bytes 130000 | tf_op jit(solution)/shard_map/choose/pallas_call | solution.py:222
  (10 shorter events, 0.1 us)
Async XLA Ops:
  0.6 21.0 %copy-start.3 = (f32[256]{0:T(256)S(1)}, f32[256]{0:T(256)}, u32[]{:S(2)}) copy-start(f32[256]{0:T(256)} %param.8) | copy-start | bytes 3076
  0.6 9.3 %collective-permute-start.2 = (f32[256,128]{1,0:T(8,128)}, f32[256,128]{1,0:T(8,128)S(1)}, u32[]{:S(2)}, u32[]{:S(2)}) collective-permute-start(f32[256,128]{1,0:T(8,128)} %own_ref.1), channel_id=1, source_target_pairs={{4,0},{5,1},{6,2},{7,3},{8,4},{9,5},{10,6},{11,7},{12,8},{13,9},{1... | collective-permute-start | bytes 393224 | tf_op jit(solution)/shard_map/ppermute | solution.py:134
  5.7 8.1 %collective-permute-start.3 = (f32[256,128]{1,0:T(8,128)}, f32[256,128]{1,0:T(8,128)S(1)}, u32[]{:S(2)}, u32[]{:S(2)}) collective-permute-start(f32[256,128]{1,0:T(8,128)} %own_ref.1), channel_id=1, source_target_pairs={{12,0},{13,1},{14,2},{15,3},{0,4},{1,5},{2,6},{3,7},{4,8},{5,9},{6... | collective-permute-start | bytes 393224 | tf_op jit(solution)/shard_map/ppermute | solution.py:134
  5.7 15.9 %collective-permute-start = (f32[256,128]{1,0:T(8,128)}, f32[256,128]{1,0:T(8,128)S(1)}, u32[]{:S(2)}, u32[]{:S(2)}) collective-permute-start(f32[256,128]{1,0:T(8,128)} %own_ref.1), channel_id=1, source_target_pairs={{1,0},{2,1},{3,2},{4,3},{5,4},{6,5},{7,6},{8,7},{9,8},{10,9},{11,1... | collective-permute-start | bytes 393224 | tf_op jit(solution)/shard_map/ppermute | solution.py:134
  9.4 12.2 %collective-permute-start.1 = (f32[256,128]{1,0:T(8,128)}, f32[256,128]{1,0:T(8,128)S(1)}, u32[]{:S(2)}, u32[]{:S(2)}) collective-permute-start(f32[256,128]{1,0:T(8,128)} %own_ref.1), channel_id=1, source_target_pairs={{15,0},{0,1},{1,2},{2,3},{3,4},{4,5},{5,6},{6,7},{7,8},{8,9},{9,10... | collective-permute-start | bytes 393224 | tf_op jit(solution)/shard_map/ppermute | solution.py:134
  9.4 13.2 %collective-permute-start.4 = (f32[256,128]{1,0:T(8,128)}, f32[256,128]{1,0:T(8,128)S(1)}, u32[]{:S(2)}, u32[]{:S(2)}) collective-permute-start(f32[256,128]{1,0:T(8,128)} %own_ref.1), channel_id=1, source_target_pairs={{8,0},{9,1},{10,2},{11,3},{12,4},{13,5},{14,6},{15,7},{0,8},{1,9},... | collective-permute-start | bytes 393224 | tf_op jit(solution)/shard_map/ppermute | solution.py:134
  10.0 12.7 %collective-permute-start.5 = (f32[256,128]{1,0:T(8,128)S(1)}, f32[256,128]{1,0:T(8,128)S(1)}, u32[]{:S(2)}, u32[]{:S(2)}) collective-permute-start(f32[256,128]{1,0:T(8,128)S(1)} %collective-permute-done.2.refs_2_), channel_id=1, source_target_pairs={{1,0},{2,1},{3,2},{4,3},{5,4},{6,5},{7,6},{8,7},{9,8},{10,9},{11,1... | collective-permute-start | bytes 393224 | tf_op jit(solution)/shard_map/ppermute | solution.py:134
  13.9 8.8 %collective-permute-start.6 = (f32[256,128]{1,0:T(8,128)S(1)}, f32[256,128]{1,0:T(8,128)S(1)}, u32[]{:S(2)}, u32[]{:S(2)}) collective-permute-start(f32[256,128]{1,0:T(8,128)S(1)} %collective-permute-done.3.refs_3_), channel_id=1, source_target_pairs={{15,0},{0,1},{1,2},{2,3},{3,4},{4,5},{5,6},{6,7},{7,8},{8,9},{9,10... | collective-permute-start | bytes 393224 | tf_op jit(solution)/shard_map/ppermute | solution.py:134
  15.2 1.6 %copy-start = (f32[128,4096]{1,0:T(8,128)S(1)}, f32[128,4096]{1,0:T(8,128)}, u32[]{:S(2)}) copy-start(f32[128,4096]{1,0:T(8,128)} %blocks_ref.1) | copy-start | bytes 6291460
  16.8 0.9 %copy-start.1 = (f32[256,128]{1,0:T(8,128)S(1)}, f32[256,128]{1,0:T(8,128)}, u32[]{:S(2)}) copy-start(f32[256,128]{1,0:T(8,128)} %own_ref.1) | copy-start | bytes 393220
  17.7 4.0 %copy-start.2 = (f32[256,128]{1,0:T(8,128)S(1)}, f32[256,128]{1,0:T(8,128)}, u32[]{:S(2)}) copy-start(f32[256,128]{1,0:T(8,128)} %own_ref.1) | copy-start | bytes 393220
  23.0 1.6 %collective-permute-start.7 = (f32[128,128]{1,0:T(8,128)S(1)}, f32[128,128]{1,0:T(8,128)S(1)}, u32[]{:S(2)}, u32[]{:S(2)}) collective-permute-start(f32[128,128]{1,0:T(8,128)S(1)} %reduce_late.1), channel_id=1, source_target_pairs={{0,1},{1,0},{2,3},{3,2},{4,5},{5,4},{6,7},{7,6},{8,9},{9,8},{10,11... | collective-permute-start | bytes 196616 | tf_op jit(solution)/shard_map/ppermute | solution.py:206
  24.6 1.8 %collective-permute-start.8 = (f32[128,128]{1,0:T(8,128)S(1)}, f32[128,128]{1,0:T(8,128)S(1)}, u32[]{:S(2)}, u32[]{:S(2)}) collective-permute-start(f32[128,128]{1,0:T(8,128)S(1)} %add.44.first_ref), channel_id=1, source_target_pairs={{0,0},{1,3},{2,2},{3,1},{4,4},{5,7},{6,6},{7,5},{8,8},{9,11},{10,1... | collective-permute-start | bytes 196616 | tf_op jit(solution)/shard_map/ppermute | solution.py:206
  26.4 0.7 %collective-permute-start.9 = (f32[128,128]{1,0:T(8,128)S(1)}, f32[128,128]{1,0:T(8,128)S(1)}, u32[]{:S(2)}, u32[]{:S(2)}) collective-permute-start(f32[128,128]{1,0:T(8,128)S(1)} %add_after.1), channel_id=1, source_target_pairs={{0,0},{1,5},{2,2},{3,7},{4,4},{5,1},{6,6},{7,3},{8,8},{9,13},{10,1... | collective-permute-start | bytes 196616 | tf_op jit(solution)/shard_map/ppermute | solution.py:206
  27.1 0.7 %collective-permute-start.10 = (f32[128,128]{1,0:T(8,128)S(1)}, f32[128,128]{1,0:T(8,128)S(1)}, u32[]{:S(2)}, u32[]{:S(2)}) collective-permute-start(f32[128,128]{1,0:T(8,128)S(1)} %add.45), channel_id=1, source_target_pairs={{0,0},{1,9},{2,2},{3,11},{4,4},{5,13},{6,6},{7,15},{8,8},{9,1},{10... | collective-permute-start | bytes 196616 | tf_op jit(solution)/shard_map/ppermute | solution.py:206
  27.8 14.8 %collective-permute-start.11 = (f32[128,128]{1,0:T(8,128)S(1)}, f32[128,128]{1,0:T(8,128)S(1)}, u32[]{:S(2)}, u32[]{:S(2)}) collective-permute-start(f32[128,128]{1,0:T(8,128)S(1)} %add.46.odd_ref), channel_id=1, source_target_pairs={{0,1},{1,0},{2,3},{3,2},{4,5},{5,4},{6,7},{7,6},{8,9},{9,8},{10,11... | collective-permute-start | bytes 196616 | tf_op jit(solution)/shard_map/ppermute | solution.py:206
